TPU v7x, 32 devices: a whole 2x2x4 slice. The times are simulated.
32 devices in a mesh: grp: 2 (over y), gx: 16 (over z, x, core).
Axes of the slice: x: 2, y: 2, z: 4, core: 2. Of those that a mesh axis runs over, the one named last changes fastest.
Arguments:
- state: float32 [5, 192, 16, 128], P(None, ('grp', 'gx')), parts along dimension 1, may hold values from -7.2 to 7.2
- cotangent: float32 [5, 192, 16, 128], P(None, ('grp', 'gx')), parts along dimension 1, may hold values from -6 to 6
- weight_in: float32 [16, 128], replicated, may hold values from -1.5 to 1.5
- bias_in: float32 [128], replicated, may hold values from -3 to 3
- weight_mid: float32 [128, 128], replicated, may hold values from -0.5 to 0.5
- bias_mid: float32 [128], replicated, may hold values from -3 to 3
- weight_out: float32 [128, 6], replicated, may hold values from -0.5 to 0.5
- cell_index: int32 [2, 1024], P(None, 'grp'), parts along dimension 1, may hold values from 0 to 196607
- segment_id: int32 [2, 1024], P(None, 'grp'), parts along dimension 1, may hold values from 0 to 63
- segment_coef: float32 [64], replicated, may hold values from 0.1 to 1
Outputs:
- grad_state: float32 [5, 192, 16, 128], P(None, ('grp', 'gx')), parts along dimension 1
- grad_weight_in: float32 [32, 128], P('grp'), parts along dimension 0
- grad_bias_in: float32 [256], P('grp'), parts along dimension 0
- grad_weight_mid: float32 [256, 128], P('grp'), parts along dimension 0
- grad_bias_mid: float32 [256], P('grp'), parts along dimension 0
- grad_weight_out: float32 [256, 6], P('grp'), parts along dimension 0
There are 2 independent parts, one for each index of `grp`. A program takes and returns all parts, laid end to end along the dimension named above; an argument that names none is the same for every part. Nothing has to cross between parts.
Inputs may be any that keep to these rules, and one draw needn't show every extreme that they name: `cell_index`: flat cell indices; a cell may appear more than once.
All inputs are finite; a program needn't handle non-finite values.
Results may differ from a plain program's by a relative error of at most 0.000098.
Values sent between devices are 32-bit elements; how exact they have to be, the bound alone decides.
A program may use at most 64 MiB of HBM per device.

v0:
```python
import math

import jax
import jax.numpy as jnp
from jax import lax
from jax.sharding import PartitionSpec as P

MEAN_WIND = 0.5
TIME_STEP = 0.2
CLOSURE_SCALE = 0.1
EPSILON = 1e-05
HIGHEST_PRECISION = lax.Precision.HIGHEST


def extended(cells, sides, width):
    for axis, dim in sides:
        count = lax.axis_size(axis)
        head = lax.slice_in_dim(cells, 0, width, axis=dim)
        tail = lax.slice_in_dim(cells, cells.shape[dim] - width, cells.shape[dim], axis=dim)
        cells = jnp.concatenate(
            [
                lax.ppermute(tail, axis, [(i, (i + 1) % count) for i in range(count)]),
                cells,
                lax.ppermute(head, axis, [((i + 1) % count, i) for i in range(count)]),
            ],
            axis=dim,
        )
    return cells


def along_x(source, low_plane, high_plane):
    return (
        source[:, low_plane + 1 : high_plane + 1] - source[:, low_plane - 1 : high_plane - 1]
    ) * 0.5


def along_y(source):
    return (jnp.roll(source, -1, axis=-2) - jnp.roll(source, 1, axis=-2)) * 0.5


def along_z(source):
    return (jnp.roll(source, -1, axis=-1) - jnp.roll(source, 1, axis=-1)) * 0.5


def velocity_gradient(padded, low_plane, high_plane):
    velocity = padded[1:4]
    centre = velocity[:, low_plane:high_plane]
    return jnp.stack(
        [along_x(velocity, low_plane, high_plane), along_y(centre), along_z(centre)], axis=1
    )


def square_sum(padded, low_plane, high_plane):
    gradient = velocity_gradient(padded, low_plane, high_plane)
    return jnp.sum(gradient * gradient)


def closure_block(feature, weights):
    weight_in, bias_in, weight_mid, bias_mid, weight_out = weights
    hidden_one = jnp.tanh(
        jnp.dot(
            weight_in.T, feature, precision=HIGHEST_PRECISION, preferred_element_type=jnp.float32
        )
        + bias_in[:, None]
    )
    hidden_two = jnp.tanh(
        jnp.dot(
            weight_mid.T,
            hidden_one,
            precision=HIGHEST_PRECISION,
            preferred_element_type=jnp.float32,
        )
        + bias_mid[:, None]
    )
    return CLOSURE_SCALE * jnp.dot(
        weight_out.T, hidden_two, precision=HIGHEST_PRECISION, preferred_element_type=jnp.float32
    )


def subgrid_stress(padded, scale, weights):
    planes = padded.shape[1]
    span_y = padded.shape[2]
    span_z = padded.shape[3]
    count = planes - 4
    gradient = velocity_gradient(padded, 2, planes - 2) / scale
    strain = 0.5 * (gradient + jnp.swapaxes(gradient, 0, 1))
    spin = 0.5 * (gradient - jnp.swapaxes(gradient, 0, 1))
    centre = padded[:, 2 : planes - 2]
    stacked = jnp.concatenate(
        [
            gradient.reshape(9, count, span_y, span_z),
            centre[1:4],
            centre[0:1],
            centre[4:5],
            jnp.sum(strain * strain, axis=(0, 1))[None],
            jnp.sum(spin * spin, axis=(0, 1))[None],
        ],
        axis=0,
    )
    feature = jnp.transpose(stacked.reshape(16, count, span_y * span_z), (1, 0, 2))
    saved = jax.checkpoint(closure_block)
    stress = lax.map(lambda block: saved(block, weights), feature)
    return jnp.transpose(stress, (1, 0, 2)).reshape(6, count, span_y, span_z)


def forcing(velocity_x, cell_index, segment_id, segment_coef, start, total):
    count = velocity_x.shape[0]
    plane_cells = velocity_x.shape[1] * velocity_x.shape[2]
    plane = cell_index // plane_cells
    local = (plane - start) % total
    inside = local < count
    flat = jnp.where(inside, local * plane_cells + cell_index % plane_cells, count * plane_cells)
    speed = MEAN_WIND + jnp.take(velocity_x.reshape(-1), flat, mode="clip")
    selector = (
        segment_id[:, None] == jnp.arange(segment_coef.shape[0], dtype=jnp.int32)[None, :]
    ).astype(jnp.float32)
    coefficient = jnp.dot(
        selector, segment_coef, precision=HIGHEST_PRECISION, preferred_element_type=jnp.float32
    )
    thrust = -coefficient * speed * jnp.abs(speed)
    empty = jnp.zeros((count * plane_cells,), jnp.float32)
    return empty.at[flat].add(thrust, mode="drop").reshape(velocity_x.shape)


def tendency(padded, scale, weights, cell_index, segment_id, segment_coef, start, total):
    planes = padded.shape[1]
    stress = subgrid_stress(padded, scale, weights)
    middle = stress[:, 1:-1]

    def stress_x(entry):
        return (stress[entry, 2:] - stress[entry, :-2]) * 0.5

    subgrid_x = stress_x(0) + along_y(middle[3]) + along_z(middle[4])
    subgrid_y = stress_x(3) + along_y(middle[1]) + along_z(middle[5])
    subgrid_z = stress_x(4) + along_y(middle[5]) + along_z(middle[2])
    centre = padded[:, 3 : planes - 3]
    upwind = (
        2.0 * padded[:, 4 : planes - 2]
        + 3.0 * centre
        - 6.0 * padded[:, 2 : planes - 4]
        + padded[:, 1 : planes - 5]
    ) / 6.0
    pressure_x = along_x(padded[4:5], 3, planes - 3)[0]
    divergence = along_x(padded[1:2], 3, planes - 3)[0] + along_y(centre[2]) + along_z(centre[3])
    thrust = forcing(centre[1], cell_index, segment_id, segment_coef, start, total)
    advect = -MEAN_WIND * upwind
    return jnp.stack(
        [
            advect[0] - divergence,
            advect[1] - pressure_x + subgrid_x + thrust,
            advect[2] - along_y(centre[4]) + subgrid_y,
            advect[3] - along_z(centre[4]) + subgrid_z,
            advect[4] - divergence,
        ],
        axis=0,
    )


def shards(
    state,
    cotangent,
    weight_in,
    bias_in,
    weight_mid,
    bias_mid,
    weight_out,
    cell_index,
    segment_id,
    segment_coef,
):
    weights = (weight_in, bias_in, weight_mid, bias_mid, weight_out)
    planes = state.shape[1]
    total = planes * lax.axis_size("gx")
    cells = total * state.shape[2] * state.shape[3]
    anchor = lax.axis_index("gx") * planes

    def scale_of(padded, depth):
        partial_sum = square_sum(padded, depth, padded.shape[1] - depth)
        summed = lax.psum(partial_sum, "gx")
        return jnp.sqrt(summed / cells + EPSILON)

    def section(padded, depth, slot):
        scale = scale_of(padded, depth)
        start = anchor - depth + 3

        def local_rate(source, params):
            return tendency(
                source,
                scale,
                params,
                cell_index[slot],
                segment_id[slot],
                segment_coef,
                start,
                total,
            )

        return jax.vjp(local_rate, padded, weights)

    def fold(gradient, depth):
        width = gradient.shape[1]
        rims = jnp.concatenate([gradient[:, :depth], gradient[:, width - depth :]], axis=1)
        widened = extended(rims, (("gx", 1),), depth)
        owned = gradient[:, depth : width - depth]
        owned = owned.at[:, :depth].add(widened[:, :depth])
        return owned.at[:, planes - depth :].add(widened[:, 3 * depth :])

    def extend(current):
        return extended(current, (("gx", 1),), 3)

    padded_zero = extend(state)
    rate_zero, pull_zero = section(padded_zero, 3, 0)
    middle = state + TIME_STEP * rate_zero
    rate_one, pull_one = section(extend(middle), 3, 1)
    back_one, grads_one = pull_one(0.25 * TIME_STEP * cotangent)
    carried = 0.25 * cotangent + fold(back_one, 3)
    back_zero, grads_zero = pull_zero(TIME_STEP * carried)
    grad_state = 0.75 * cotangent + carried + fold(back_zero, 3)
    totals = lax.psum(
        (
            grads_zero[0] + grads_one[0],
            grads_zero[1] + grads_one[1],
            grads_zero[2] + grads_one[2],
            grads_zero[3] + grads_one[3],
            grads_zero[4] + grads_one[4],
        ),
        "gx",
    )
    factor = 1.0 / (TIME_STEP * CLOSURE_SCALE * math.sqrt(cells))
    return (
        grad_state,
        totals[0] * factor,
        totals[1] * factor,
        totals[2] * factor,
        totals[3] * factor,
        totals[4] * factor,
    )


def solution(mesh):
    return jax.shard_map(
        shards,
        mesh=mesh,
        in_specs=(
            P(None, ("grp", "gx"), None, None),
            P(None, ("grp", "gx"), None, None),
            P(),
            P(),
            P(),
            P(),
            P(),
            P(None, "grp"),
            P(None, "grp"),
            P(),
        ),
        out_specs=(
            P(None, ("grp", "gx"), None, None),
            P("grp", None),
            P("grp"),
            P("grp", None),
            P("grp"),
            P("grp", None),
        ),
        check_vma=False,
    )
```

profile of v0, /device:TPU:0, one launch (start us, length us, event | category | flops | bytes accessed | tf_op | source)
XLA Modules:
  0.0 614.2 jit_solution(10288684754206381452)
XLA Ops:
  9.5 5.0 collective-permute-start
  44.8 3.1 gather_fusion
  58.6 4.0 scatter_custom_fusion
  62.6 4.3 gather_fusion.2
  77.5 30.9 %psum.49 = f32[]{:T(128)} all-reduce(f32[]{:T(128)} %fusion.29), channel_id=1, replica_groups=mesh['grp'=2,'gx'=16] {'gx'}, use_global_device_ids=true, to_apply=%region_1.2 | all-reduce | flops 1 | bytes 8 | tf_op jit(solution)/shard_map/psum | solution.py:179
  111.9 2.0 div.88
  116.5 35.6 %while.64 = (s32[]{:T(128)}, f32[8,6,2048]{2,1,0:T(8,128)}, f32[8,16,2048]{2,1,0:T(8,128)S(1)}, f32[128,16]{0,1:T(8,128)S(1)}, f32[128,1]{0,1:T(1,128)S(1)}, /*i...) while((s32[]{:T(128)}, f32[8,6,2048]{2,1,0:T(8,128)}, ...), condition=%wide.region_5.6_spmd, body=%wide.region_4.5_spmd.sunk | while | flops 472395776 | bytes 4468845 | solution.py:102
  116.5 1.8 fusion.304
  121.0 1.8 fusion.304
  125.4 1.8 fusion.304
  129.9 1.8 fusion.304
  134.3 1.8 fusion.304
  138.8 1.8 fusion.304
  143.2 1.8 fusion.304
  152.1 2.3 reshape.1759
  174.9 4.4 collective-permute-start.2
  179.4 3.1 gather_fusion.1
  183.3 4.1 scatter_custom_fusion.1
  188.3 2.0 broadcast_multiply_fusion.3
  196.4 30.4 %psum.50 = f32[]{:T(128)} all-reduce(f32[]{:T(128)} %fusion.30), channel_id=1, replica_groups=mesh['grp'=2,'gx'=16] {'gx'}, use_global_device_ids=true, to_apply=%region_9.10 | all-reduce | flops 1 | bytes 8 | tf_op jit(solution)/shard_map/psum | solution.py:179
  230.9 2.0 div.99
  235.1 83.7 %while.65 = (s32[]{:T(128)}, f32[16,128]{1,0:T(8,128)S(1)}, f32[128]{0:T(128)S(1)}, f32[128,128]{1,0:T(8,128)S(1)}, f32[128]{0:T(128)S(1)}, /*index=5*/f32[128,6...) while((s32[]{:T(128)}, f32[16,128]{1,0:T(8,128)S(1)}, ...), condition=%wide.region_15.16_spmd.clone, body=%wide.region_12.15_spmd.clone.sunk | while | flops 1399912192 | bytes 15153354 | solution.py:102
  331.6 4.9 collective-permute-start.5
  338.2 3.5 scatter-add.42
  341.8 3.5 scatter-add.43
  355.0 80.0 %while.66 = (s32[]{:T(128)}, f32[16,128]{1,0:T(8,128)S(1)}, f32[128]{0:T(128)S(1)}, f32[128,128]{1,0:T(8,128)S(1)}, f32[128]{0:T(128)S(1)}, /*index=5*/f32[128,6...) while((s32[]{:T(128)}, f32[16,128]{1,0:T(8,128)S(1)}, ...), condition=%wide.region_20.21_spmd.clone, body=%wide.region_17.20_spmd.clone.sunk | while | flops 1399912192 | bytes 14891210 | solution.py:102
  443.7 3.1 gather_fusion.3
  447.6 4.0 scatter_custom_fusion.2
  454.5 59.9 %all-reduce.176 = (f32[16,128]{1,0:T(8,128)S(1)}, f32[128]{0:T(128)S(1)}, f32[128]{0:T(128)S(1)}, f32[128,6]{0,1:T(8,128)S(1)}) all-reduce(f32[16,128]{1,0:T(8,128)S(1)} %add.932, f32[128]{0:T(128)S(1)} %add.933, f32[128]{0:T(128)S(1)} %add.935, f32[128,6]{0,1:T(8,128)S(1)} %add.936), channel_id=1, replica_groups=mesh['grp'=2,'gx'=16] {'gx'}, use_global_device_ids=true, to_apply=%region_21.22 | all-reduce | flops 3072 | bytes 24576 | tf_op jit(solution)/shard_map/psum | solution.py:219
  528.8 68.9 %all-reduce.179.cloned.1.call-done = f32[128,128]{1,0:T(8,128)} async-done(((f32[128,128]{1,0:T(8,128)}), f32[128,128]{1,0:T(8,128)}) %all-reduce.179.cloned.1.call-update) | async-done | bytes 65552 | tf_op jit(solution)/shard_map/psum | solution.py:219
  599.2 3.5 scatter-add.45
  602.8 3.5 scatter-add.46
  (904 shorter events, 330.1 us)
Async XLA Ops:
  7.2 28.5 %copy-start = (f32[64]{0:T(128)S(1)}, f32[64]{0:T(128)}, u32[]{:S(2)}) copy-start(f32[64]{0:T(128)} %param.33) | copy-start | bytes 772
  7.2 590.5 %all-reduce.179.cloned.1.call-start = ((), (), s32[]{:S(2)}) async-start(), calls=%async_computation | async-start | bytes 131072 | tf_op jit(solution)/shard_map/psum | solution.py:219
  8.3 6.2 %copy-start.2 = (f32[5,6,16,128]{3,2,1,0:T(8,128)S(1)}, f32[5,6,16,128]{3,2,1,0:T(8,128)}, u32[]{:S(2)}) copy-start(f32[5,6,16,128]{3,2,1,0:T(8,128)} %param.24) | copy-start | bytes 737284
  9.1 58.7 %collective-permute-start.1 = (f32[5,3,16,128]{3,1,2,0:T(4,128)}, f32[5,3,16,128]{3,1,2,0:T(4,128)S(1)}, u32[]{:S(2)}, u32[]{:S(2)}) collective-permute-start(f32[5,3,16,128]{3,1,2,0:T(4,128)} %get-tuple-element.1100), channel_id=1, source_target_pairs={{0,1},{1,2},{2,3},{3,4},{4,5},{5,6},{6,7},{7,8},{8,9},{9,10},{10,1... | collective-permute-start | bytes 368648 | tf_op jit(solution)/shard_map/ppermute | solution.py:22
  9.5 58.3 %collective-permute-start = (f32[5,3,16,128]{3,1,2,0:T(4,128)}, f32[5,3,16,128]{3,1,2,0:T(4,128)S(1)}, u32[]{:S(2)}, u32[]{:S(2)}) collective-permute-start(f32[5,3,16,128]{3,1,2,0:T(4,128)} %get-tuple-element.1101), channel_id=1, source_target_pairs={{1,0},{2,1},{3,2},{4,3},{5,4},{6,5},{7,6},{8,7},{9,8},{10,9},{11,1... | collective-permute-start | bytes 368648 | tf_op jit(solution)/shard_map/ppermute | solution.py:24
  19.7 22.9 %copy-start.43 = (f32[6,16,128]{2,0,1:T(8,128)}, f32[6,16,128]{2,0,1:T(8,128)S(1)}, u32[]{:S(2)}) copy-start(f32[6,16,128]{2,0,1:T(8,128)S(1)} %get-tuple-element.1078) | copy-start | bytes 147460
  26.5 22.7 %copy-start.35 = (f32[1,6,16,128]{3,1,2,0:T(8,128)}, f32[1,6,16,128]{3,1,2,0:T(8,128)S(1)}, u32[]{:S(2)}) copy-start(f32[1,6,16,128]{3,1,2,0:T(8,128)S(1)} %get-tuple-element.1073) | copy-start | bytes 147460
  26.5 22.7 %copy-start.37 = (f32[1,6,16,128]{3,1,2,0:T(8,128)}, f32[1,6,16,128]{3,1,2,0:T(8,128)S(1)}, u32[]{:S(2)}) copy-start(f32[1,6,16,128]{3,1,2,0:T(8,128)S(1)} %get-tuple-element.1077) | copy-start | bytes 147460
  36.6 4.0 copy-start.123
  38.1 4.4 copy-start.4
  44.7 3.2 copy-start.158
  44.7 3.8 copy-start.75
  44.7 3.8 copy-start.76
  44.8 3.8 copy-start.77
  58.5 4.1 copy-start.155
  76.6 32.5 %copy-start.27 = (f32[3,1,8,16,1]{4,2,0,3,1:T(8,128)S(1)}, f32[3,1,8,16,1]{4,2,0,3,1:T(8,128)}, u32[]{:S(2)}) copy-start(f32[3,1,8,16,1]{4,2,0,3,1:T(8,128)} %copy.175) | copy-start | bytes 4612
  152.1 4.0 copy-start.6
  163.9 3.3 copy-start.71
  163.9 5.1 copy-start.47
  164.0 5.0 copy-start.13
  174.9 4.5 copy-start.154
  174.9 17.1 %collective-permute-start.3 = (f32[5,3,16,128]{3,1,2,0:T(4,128)}, f32[5,3,16,128]{3,1,2,0:T(4,128)S(1)}, u32[]{:S(2)}, u32[]{:S(2)}) collective-permute-start(f32[5,3,16,128]{3,1,2,0:T(4,128)} %get-tuple-element.1091), channel_id=1, source_target_pairs={{0,1},{1,2},{2,3},{3,4},{4,5},{5,6},{6,7},{7,8},{8,9},{9,10},{10,1... | collective-permute-start | bytes 368648 | tf_op jit(solution)/shard_map/ppermute | solution.py:22
  174.9 17.0 %collective-permute-start.2 = (f32[5,3,16,128]{3,1,2,0:T(4,128)}, f32[5,3,16,128]{3,1,2,0:T(4,128)S(1)}, u32[]{:S(2)}, u32[]{:S(2)}) collective-permute-start(f32[5,3,16,128]{3,1,2,0:T(4,128)} %get-tuple-element.1092), channel_id=1, source_target_pairs={{1,0},{2,1},{3,2},{4,3},{5,4},{6,5},{7,6},{8,7},{9,8},{10,9},{11,1... | collective-permute-start | bytes 368648 | tf_op jit(solution)/shard_map/ppermute | solution.py:24
  179.4 3.2 copy-start.168
  179.4 8.1 %copy-start.72 = (f32[1,6,16,128]{3,1,2,0:T(8,128)S(1)}, f32[1,6,16,128]{3,1,2,0:T(8,128)}, u32[]{:S(2)}) copy-start(f32[1,6,16,128]{3,1,2,0:T(8,128)} %get-tuple-element.1168) | copy-start | bytes 147460
  179.4 8.1 %copy-start.73 = (f32[1,6,16,128]{3,1,2,0:T(8,128)S(1)}, f32[1,6,16,128]{3,1,2,0:T(8,128)}, u32[]{:S(2)}) copy-start(f32[1,6,16,128]{3,1,2,0:T(8,128)} %get-tuple-element.1169) | copy-start | bytes 147460
  179.4 8.1 %copy-start.74 = (f32[1,6,16,128]{3,1,2,0:T(8,128)S(1)}, f32[1,6,16,128]{3,1,2,0:T(8,128)}, u32[]{:S(2)}) copy-start(f32[1,6,16,128]{3,1,2,0:T(8,128)} %get-tuple-element.1166) | copy-start | bytes 147460
  183.3 4.2 copy-start.38
  330.6 7.6 %collective-permute-start.4 = (f32[5,3,16,128]{3,1,2,0:T(4,128)S(1)}, f32[5,3,16,128]{3,1,2,0:T(4,128)S(1)}, u32[]{:S(2)}, u32[]{:S(2)}) collective-permute-start(f32[5,3,16,128]{3,1,2,0:T(4,128)S(1)} %get-tuple-element.984), channel_id=1, source_target_pairs={{0,1},{1,2},{2,3},{3,4},{4,5},{5,6},{6,7},{7,8},{8,9},{9,10},{10,1... | collective-permute-start | bytes 368648 | tf_op jit(solution)/shard_map/ppermute | solution.py:22
  331.6 10.1 %collective-permute-start.5 = (f32[5,3,16,128]{3,1,2,0:T(4,128)S(1)}, f32[5,3,16,128]{3,1,2,0:T(4,128)S(1)}, u32[]{:S(2)}, u32[]{:S(2)}) collective-permute-start(f32[5,3,16,128]{3,1,2,0:T(4,128)S(1)} %get-tuple-element.983), channel_id=1, source_target_pairs={{1,0},{2,1},{3,2},{4,3},{5,4},{6,5},{7,6},{8,7},{9,8},{10,9},{11,1... | collective-permute-start | bytes 368648 | tf_op jit(solution)/shard_map/ppermute | solution.py:24
  528.2 74.5 %collective-permute-start.7 = (f32[5,3,16,128]{3,1,2,0:T(4,128)S(1)}, f32[5,3,16,128]{3,1,2,0:T(4,128)S(1)}, u32[]{:S(2)}, u32[]{:S(2)}) collective-permute-start(f32[5,3,16,128]{3,1,2,0:T(4,128)S(1)} %get-tuple-element.981), channel_id=1, source_target_pairs={{1,0},{2,1},{3,2},{4,3},{5,4},{6,5},{7,6},{8,7},{9,8},{10,9},{11,1... | collective-permute-start | bytes 368648 | tf_op jit(solution)/shard_map/ppermute | solution.py:24
  528.3 70.9 %collective-permute-start.6 = (f32[5,3,16,128]{3,1,2,0:T(4,128)S(1)}, f32[5,3,16,128]{3,1,2,0:T(4,128)S(1)}, u32[]{:S(2)}, u32[]{:S(2)}) collective-permute-start(f32[5,3,16,128]{3,1,2,0:T(4,128)S(1)} %get-tuple-element.982), channel_id=1, source_target_pairs={{0,1},{1,2},{2,3},{3,4},{4,5},{5,6},{6,7},{7,8},{8,9},{9,10},{10,1... | collective-permute-start | bytes 368648 | tf_op jit(solution)/shard_map/ppermute | solution.py:22
  (151 other events, 139.5 us)
Sparse Core Ops, SparseCore 0:
  515.8 81.8 all-reduce.178
where the time goes:
time: 625 us; the launch traced here: 614 us
  local copies, waits for them, and re-layouts  175 us (28%)
  matrix products  165 us (26%)
  blocking collectives  121 us (19%)
  waiting for transfers between devices  70.7 us (11%)
  other arithmetic  47.9 us (8%)
  between operations  17.7 us (3%)
  starting transfers between devices  15.4 us (2%)
    psum x1, waiting for transfers between devices, shards(): lax.psum((grads_zero[0] + grads_one[0], grads_zero[1] + grads_one[1], gra...  68.9 us
    psum x2, blocking collectives, scale_of(): summed = lax.psum(partial_sum, 'gx')  61.3 us
    psum x1, blocking collectives, shards(): lax.psum((grads_zero[0] + grads_one[0], grads_zero[1] + grads_one[1], gra...  59.9 us
    dot_general x56, matrix products, closure_block(): jnp.dot(weight_mid.T, hidden_one, precision=HIGHEST_PRECISION, preferred_...  59.8 us
    dot_general x56, matrix products, closure_block(): jnp.dot(weight_in.T, feature, precision=HIGHEST_PRECISION, preferred_elem...  56.1 us
    dot_general x40, matrix products, closure_block(): jnp.dot(weight_out.T, hidden_two, precision=HIGHEST_PRECISION, preferred_...  46.8 us
    unnamed x357, local copies, waits for them, and re-layouts  40.9 us
    dynamic_slice x48, local copies, waits for them, and re-layouts, subgrid_stress(): stress = lax.map(lambda block: saved(block, weights), feature)  27.8 us
  transfers between devices with their start and end apart: 9, of which 2 were waited for; matrix products, arithmetic and copies ran while one was open for 11% of the time, Pallas kernels for 0%

commit v1 on v0

v1 whole, which is shorter than its diff:
```python
import functools
import math

import jax
import jax.numpy as jnp
from jax import lax
from jax.experimental import pallas as pl
from jax.experimental.pallas import tpu as pltpu
from jax.sharding import PartitionSpec as P

MEAN_WIND = 0.5
TIME_STEP = 0.2
CLOSURE_SCALE = 0.1
EPSILON = 1e-05
F32 = jnp.float32
BF16 = jnp.bfloat16
ROWS = 8
GROUP = 16
MESH = pl.DeviceIdType.MESH


def split(value):
    high = value.astype(BF16)
    return high, (value - high.astype(F32)).astype(BF16)


def dot(left, right):
    return jnp.dot(left, right, preferred_element_type=F32)


def dot_nt(left, right):
    return lax.dot_general(left, right, (((1,), (1,)), ((), ())), preferred_element_type=F32)


def along_y(field):
    return (pltpu.roll(field, field.shape[1] - 1, 1) - pltpu.roll(field, 1, 1)) * 0.5


def along_z(field):
    return (pltpu.roll(field, field.shape[2] - 1, 2) - pltpu.roll(field, 1, 2)) * 0.5


def kernel(
    count,
    cells,
    state,
    cotangent,
    weight_in,
    bias_in,
    weight_mid,
    bias_mid,
    weight_out,
    cell_index,
    segment_id,
    segment_coef,
    grad_state,
    grad_in,
    grad_bias_in,
    grad_mid,
    grad_bias_mid,
    grad_out,
    pad_state,
    pad_middle,
    pad_cot,
    pad_carry,
    pad_stress,
    pad_grad,
    send_stress,
    send_grad,
    feats,
    stress,
    dstress,
    dfeats,
    hidden_one,
    hidden_two,
    left_one,
    left_mid,
    left_stress,
    left_out,
    left_back,
    left_feat,
    bias_two,
    acc_mid,
    acc_in,
    acc_out,
    sum_slots,
    sum_far,
    grad_parts,
    grad_slots,
    grad_total,
    grad_far,
    halo_send,
    halo_recv,
    sum_send,
    sum_recv,
    red_send,
    red_recv,
    gat_send,
    gat_recv,
    far_send,
    far_recv,
):
    planes = state.shape[1]
    span = state.shape[2]
    lanes = state.shape[3]
    rows = planes * span
    wide = ROWS * lanes
    per_plane = span // ROWS
    hid = weight_mid.shape[0]
    far = count // GROUP
    me = lax.axis_index("gx")
    mine = lax.rem(me, GROUP)
    base = me - mine
    block = me // GROUP
    right = lax.rem(me + 1, count)
    left = lax.rem(me + count - 1, count)

    def mate(step):
        return lax.rem(mine + step, GROUP)

    def far_mate(step):
        return lax.rem(block + step, far)

    barrier = pltpu.get_barrier_semaphore()
    for peer in (left, right):
        pl.semaphore_signal(barrier, inc=1, device_id={"gx": peer}, device_id_type=MESH)
    for step in range(1, GROUP):
        pl.semaphore_signal(barrier, inc=1, device_id={"gx": base + mate(step)}, device_id_type=MESH)
    for step in range(1, far):
        pl.semaphore_signal(
            barrier, inc=1, device_id={"gx": far_mate(step) * GROUP + mine}, device_id_type=MESH
        )
    pl.semaphore_wait(barrier, 2 + GROUP - 1 + far - 1)

    def remote(source, target, send, recv, peer):
        copy = pltpu.make_async_remote_copy(
            src_ref=source,
            dst_ref=target,
            send_sem=send,
            recv_sem=recv,
            device_id={"gx": peer},
            device_id_type=MESH,
        )
        copy.start()
        return copy

    def exchange(slot, to_right, at_low, to_left, at_high):
        return (
            remote(to_right, at_low, halo_send.at[slot, 0], halo_recv.at[slot, 0], right),
            remote(to_left, at_high, halo_send.at[slot, 1], halo_recv.at[slot, 1], left),
        )

    def finish(copies):
        for copy in copies:
            copy.wait()

    def halo(slot, source, start, target, low, high):
        return exchange(
            slot,
            source.at[:, start + planes - low : start + planes],
            target.at[:, 0:low],
            source.at[:, start : start + high],
            target.at[:, low + planes : low + planes + high],
        )

    state_copies = halo(0, state, 0, pad_state, 2, 1)
    cot_copies = halo(1, cotangent, 0, pad_cot, 1, 2)
    pad_state[:, 2 : 2 + planes] = state[...]
    pad_cot[:, 1 : 1 + planes] = cotangent[...]

    zeros_tail = jnp.zeros((8, lanes), F32)
    pack = jnp.concatenate(
        [weight_in[...], bias_in[...], bias_mid[...], weight_out[...], zeros_tail], axis=0
    )
    pack_high, pack_low = split(pack)
    high = pack_high.astype(F32)
    low = pack_low.astype(F32)

    def turned(parts):
        used = sum(part.shape[0] for part in parts)
        return jnp.concatenate(parts + [jnp.zeros((hid - used, lanes), F32)], axis=0).T.astype(BF16)

    left_one[...] = turned([high[:16], high[:16], low[:16], high[16:], low[16:]])
    left_stress[...] = turned([high[16:], high[16:], low[16:]])

    def stacked(value_high, value_low):
        return jnp.concatenate(
            [
                jnp.concatenate([value_high, value_high], axis=1),
                jnp.concatenate([value_low, value_low], axis=1),
            ],
            axis=0,
        )

    left_mid[...] = stacked(*split(weight_mid[...].T))
    left_back[...] = stacked(*split(weight_mid[...]))
    left_out[...] = stacked(pack_high[16:], pack_low[16:])
    left_feat[...] = stacked(pack_high[:16], pack_low[:16])
    turned_bias = jnp.concatenate([bias_mid[...], jnp.zeros((hid - 1, lanes), F32)], axis=0).T
    bias_two[...] = jnp.broadcast_to(turned_bias[:, 0:1], (hid, lanes))
    first_row = lax.broadcasted_iota(jnp.int32, (16, wide), 0) == 0
    ones_row = jnp.where(first_row, 1.0, 0.0).astype(BF16)

    def cell_coefficient(slot):
        index = cell_index[slot : slot + 1, :]
        points = index.shape[1]
        segments = segment_coef.shape[1]
        chosen = (
            lax.broadcasted_iota(jnp.int32, (segments, points), 0) == segment_id[slot : slot + 1, :]
        )
        picked = jnp.where(chosen, 1.0, 0.0)
        coef = lax.dot(
            jnp.broadcast_to(segment_coef[...], (8, segments)),
            picked,
            precision=lax.Precision.HIGHEST,
            preferred_element_type=F32,
        )[0:1]
        row = lax.div(index, jnp.int32(lanes)) - me * rows
        lane = lax.rem(index, jnp.int32(lanes))
        at_row = jnp.where(lax.broadcasted_iota(jnp.int32, (rows, points), 0) == row, 1.0, 0.0)
        at_lane = jnp.where(lax.broadcasted_iota(jnp.int32, (lanes, points), 0) == lane, coef, 0.0)
        return lax.dot_general(
            at_row,
            at_lane,
            (((1,), (1,)), ((), ())),
            precision=lax.Precision.HIGHEST,
            preferred_element_type=F32,
        ).reshape(planes, span, lanes)

    coef_zero = cell_coefficient(0)
    coef_one = cell_coefficient(1)
    acc_mid[...] = jnp.zeros_like(acc_mid)
    acc_in[...] = jnp.zeros_like(acc_in)
    acc_out[...] = jnp.zeros_like(acc_out)
    dstress[...] = jnp.zeros_like(dstress)

    def shifted(ref, comp, low, shift):
        return ref[comp, low + shift : low + shift + planes]

    def along_x(ref, comp, low):
        return (shifted(ref, comp, low, 1) - shifted(ref, comp, low, -1)) * 0.5

    def gradients(ref):
        table = []
        for comp in (1, 2, 3):
            centre = shifted(ref, comp, 2, 0)
            table.append([along_x(ref, comp, 2), along_y(centre), along_z(centre)])
        return table

    def scale_start(slot, table):
        total = None
        for line in table:
            for entry in line:
                total = entry * entry if total is None else total + entry * entry
        total = jnp.sum(total, axis=0)
        total = jnp.sum(total, axis=0, keepdims=True)
        sum_slots[slot, mine] = total
        return [
            remote(
                sum_slots.at[slot, mine],
                sum_slots.at[slot, mine],
                sum_send.at[slot, step],
                sum_recv.at[slot, step],
                base + mate(step),
            )
            for step in range(1, GROUP)
        ]

    def wait_sums(slot, copies):
        for step, copy in zip(range(1, GROUP), copies):
            copy.wait_send()
            source = mate(GROUP - step)
            pltpu.make_async_remote_copy(
                src_ref=sum_slots.at[slot, source],
                dst_ref=sum_slots.at[slot, source],
                send_sem=sum_send.at[slot, step],
                recv_sem=sum_recv.at[slot, step],
                device_id={"gx": base + mate(step)},
                device_id_type=MESH,
            ).wait_recv()

    def scale_finish(slot, copies):
        wait_sums(slot, copies)
        total = jnp.sum(sum_slots[slot], axis=0)
        if far > 1:
            sum_far[slot, 0] = total
            others = [
                remote(
                    sum_far.at[slot, 0],
                    sum_far.at[slot, step],
                    far_send.at[slot, step],
                    far_recv.at[slot, step],
                    far_mate(step) * GROUP + mine,
                )
                for step in range(1, far)
            ]
            finish(others)
            total = jnp.sum(sum_far[slot], axis=0)
        total = jnp.sum(total, axis=1, keepdims=True)
        return lax.rsqrt(total / cells + EPSILON).reshape(1, 1, 1)

    def put(ref, slot, width, value):
        ref[pl.ds(slot, rows, stride=width), :] = value.reshape(rows, lanes)

    def get(ref, slot, width, plane=0, number=planes):
        start = plane * span * width + slot
        return ref[pl.ds(start, number * span, stride=width), :].reshape(number, span, lanes)

    def write_features(section, ref, table, inverse):
        target = feats.at[section]
        scaled = [[entry * inverse for entry in line] for line in table]
        sym = None
        skew = None
        for a in range(3):
            for b in range(3):
                put(target, 3 * a + b, 16, scaled[a][b])
                plus = 0.5 * (scaled[a][b] + scaled[b][a])
                minus = 0.5 * (scaled[a][b] - scaled[b][a])
                sym = plus * plus if sym is None else sym + plus * plus
                if a != b:
                    skew = minus * minus if skew is None else skew + minus * minus
        for slot, comp in enumerate((1, 2, 3, 0, 4)):
            put(target, 9 + slot, 16, shifted(ref, comp, 2, 0))
        put(target, 14, 16, sym)
        put(target, 15, 16, skew)

    def columns(ref, chunk, height):
        start = chunk * (ROWS * height)
        return jnp.concatenate(
            [
                ref[pl.ds(pl.multiple_of(start + row * height, 8), height), :]
                for row in range(ROWS)
            ],
            axis=1,
        )

    def spread(ref, chunk, height, value):
        start = chunk * (ROWS * height)
        for row in range(ROWS):
            ref[pl.ds(pl.multiple_of(start + row * height, 8), height), :] = value[
                :height, row * lanes : (row + 1) * lanes
            ]

    def halves(value):
        size = value.shape[0] // 2
        return value[:size] + value[size:]

    def forward(section, chunk):
        feat_high, feat_low = split(columns(feats.at[section], chunk, 16))
        blank = jnp.zeros((hid - 80, wide), BF16)
        one = jnp.tanh(
            dot(
                left_one[...],
                jnp.concatenate([feat_high, feat_low, feat_high, ones_row, ones_row, blank], axis=0),
            )
        )
        one_parts = jnp.concatenate(split(one), axis=0)
        bias = jnp.concatenate([bias_two[...]] * ROWS, axis=1)
        two = jnp.tanh(halves(dot(left_mid[...], one_parts)) + bias)
        two_parts = jnp.concatenate(split(two), axis=0)
        return (feat_high, feat_low), one, one_parts, two, two_parts

    def backward(chunk, feat, one, one_parts, two, two_parts):
        small = jnp.concatenate([columns(dstress, chunk, 8), jnp.zeros((8, wide), F32)], axis=0)
        small_high, small_low = split(small)
        blank = jnp.zeros((hid - 48, wide), BF16)
        back_two = dot(
            left_stress[...],
            jnp.concatenate([small_high, small_low, small_high, blank], axis=0),
        )
        pre_two = jnp.concatenate(split(back_two * (1.0 - two * two)), axis=0)
        back_one = halves(dot(left_back[...], pre_two))
        pre_one = jnp.concatenate(split(back_one * (1.0 - one * one)), axis=0)
        spread(dfeats, chunk, 16, halves(dot(left_feat[...], pre_one)))
        acc_mid[...] += dot_nt(jnp.concatenate([one_parts, ones_row], axis=0), pre_two)
        acc_in[...] += dot_nt(jnp.concatenate([feat[0], feat[1], ones_row], axis=0), pre_one)
        acc_out[...] += dot_nt(jnp.concatenate([small_high, small_low], axis=0), two_parts)

    def forward_zero(chunk):
        _, one, _, two, two_parts = forward(0, chunk)
        hidden_one[chunk] = one
        hidden_two[chunk] = two
        spread(stress, chunk, 8, halves(dot(left_out[...], two_parts)))

    def both_one(chunk):
        backward(chunk, *forward(1, chunk))

    def backward_zero(chunk):
        one = hidden_one[chunk]
        two = hidden_two[chunk]
        feat = split(columns(feats.at[0], chunk, 16))
        one_parts = jnp.concatenate(split(one), axis=0)
        two_parts = jnp.concatenate(split(two), axis=0)
        backward(chunk, feat, one, one_parts, two, two_parts)

    def sweep(body, between):
        edge = 2 * per_plane

        def outer(step, carry):
            body(jnp.where(step < per_plane, step, step + (planes - 2) * per_plane))
            return carry

        def inner(step, carry):
            body(step)
            return carry

        lax.fori_loop(0, edge, outer, 0)
        between()
        lax.fori_loop(per_plane, (planes - 1) * per_plane, inner, 0)

    def upwind(ref, comp):
        return (
            2.0 * shifted(ref, comp, 2, 1)
            + 3.0 * shifted(ref, comp, 2, 0)
            - 6.0 * shifted(ref, comp, 2, -1)
            + shifted(ref, comp, 2, -2)
        ) * (-MEAN_WIND / 6.0)

    def upwind_back(ref, comp):
        return (
            2.0 * shifted(ref, comp, 1, -1)
            + 3.0 * shifted(ref, comp, 1, 0)
            - 6.0 * shifted(ref, comp, 1, 1)
            + shifted(ref, comp, 1, 2)
        ) * (-MEAN_WIND / 6.0)

    def write_dstress(ref, factor):
        factor = -factor * CLOSURE_SCALE
        u, v, w = (shifted(ref, comp, 1, 0) for comp in (1, 2, 3))
        put(dstress, 2, 8, along_x(ref, 1, 1) * factor)
        put(dstress, 3, 8, along_y(v) * factor)
        put(dstress, 4, 8, along_z(w) * factor)
        put(dstress, 5, 8, (along_y(u) + along_x(ref, 2, 1)) * factor)
        put(dstress, 6, 8, (along_z(u) + along_x(ref, 3, 1)) * factor)
        put(dstress, 7, 8, (along_z(v) + along_y(w)) * factor)

    def dgradient(section, a, b, inverse, plane, number):
        ref = feats.at[section]
        total = get(dfeats, 3 * a + b, 16, plane, number)
        sym = get(dfeats, 14, 16, plane, number)
        here = get(ref, 3 * a + b, 16, plane, number)
        there = get(ref, 3 * b + a, 16, plane, number)
        total = total + (here + there) * sym
        if a != b:
            total = total + (here - there) * get(dfeats, 15, 16, plane, number)
        return total * inverse

    def send_dgradient(section, inverse):
        for a in range(3):
            send_grad[section, 0, a] = dgradient(section, a, 0, inverse, planes - 1, 1)
            send_grad[section, 1, a] = dgradient(section, a, 0, inverse, 0, 1)
        return exchange(
            5 + section,
            send_grad.at[section, 0],
            pad_grad.at[section, :, 0:1],
            send_grad.at[section, 1],
            pad_grad.at[section, :, planes + 1 : planes + 2],
        )

    def back_linear(ref, factor, speed_ref, coef):
        mass_rho = shifted(ref, 0, 1, 0) + shifted(ref, 4, 1, 0)
        mass_x = along_x(ref, 0, 1) + along_x(ref, 4, 1)
        u, v, w = (shifted(ref, comp, 1, 0) for comp in (1, 2, 3))
        speed = MEAN_WIND + shifted(speed_ref, 1, 2, 0)
        return [
            upwind_back(ref, 0) * factor,
            (upwind_back(ref, 1) + mass_x - 2.0 * coef * jnp.abs(speed) * u) * factor,
            (upwind_back(ref, 2) + along_y(mass_rho)) * factor,
            (upwind_back(ref, 3) + along_z(mass_rho)) * factor,
            (upwind_back(ref, 4) + along_x(ref, 1, 1) + along_y(v) + along_z(w)) * factor,
        ]

    def back_closure(section, inverse, linear, copies):
        for a in range(3):
            pad_grad[section, a, 1 : 1 + planes] = dgradient(section, a, 0, inverse, 0, planes)
        total = list(linear)
        for slot, comp in enumerate((1, 2, 3, 0, 4)):
            total[comp] = total[comp] + get(dfeats, 9 + slot, 16)
        for a in range(3):
            total[1 + a] = (
                total[1 + a]
                - along_y(dgradient(section, a, 1, inverse, 0, planes))
                - along_z(dgradient(section, a, 2, inverse, 0, planes))
            )
        finish(copies)
        ref = pad_grad.at[section]
        for a in range(3):
            total[1 + a] = total[1 + a] - along_x(ref, a, 1)
        return total

    finish(state_copies)
    table = gradients(pad_state)
    copies = scale_start(0, table)
    divergence = table[0][0] + table[1][1] + table[2][2]
    speed = MEAN_WIND + shifted(pad_state, 1, 2, 0)
    pressure = shifted(pad_state, 4, 2, 0)
    rate = [
        upwind(pad_state, 0) - divergence,
        upwind(pad_state, 1) - along_x(pad_state, 4, 2) - coef_zero * speed * jnp.abs(speed),
        upwind(pad_state, 2) - along_y(pressure),
        upwind(pad_state, 3) - along_z(pressure),
        upwind(pad_state, 4) - divergence,
    ]
    for comp in range(5):
        pad_middle[comp, 2 : 2 + planes] = (
            shifted(pad_state, comp, 2, 0) + TIME_STEP * rate[comp]
        )
    finish(cot_copies)
    write_dstress(pad_cot, 0.25 * TIME_STEP)
    inverse_zero = scale_finish(0, copies)
    write_features(0, pad_state, table, inverse_zero)
    stress_copies = []

    def send_edges():
        for slot, entry in enumerate((0, 3, 4)):
            send_stress[0, slot] = get(stress, 2 + entry, 8, planes - 1, 1)
            send_stress[1, slot] = get(stress, 2 + entry, 8, 0, 1)
        stress_copies.extend(
            exchange(
                2,
                send_stress.at[0],
                pad_stress.at[:, 0:1],
                send_stress.at[1],
                pad_stress.at[:, planes + 1 : planes + 2],
            )
        )

    sweep(forward_zero, send_edges)
    for slot, entry in enumerate((0, 3, 4)):
        pad_stress[slot, 1 : 1 + planes] = get(stress, 2 + entry, 8)
    s_yy, s_zz, s_xy, s_xz, s_yz = (get(stress, 2 + entry, 8) for entry in (1, 2, 3, 4, 5))
    sub_x = along_y(s_xy) + along_z(s_xz)
    sub_y = along_y(s_yy) + along_z(s_yz)
    sub_z = along_y(s_yz) + along_z(s_zz)
    finish(stress_copies)
    gain = TIME_STEP * CLOSURE_SCALE
    for slot, sub in enumerate((sub_x, sub_y, sub_z)):
        here = shifted(pad_middle, 1 + slot, 2, 0)
        pad_middle[1 + slot, 2 : 2 + planes] = here + gain * (sub + along_x(pad_stress, slot, 1))

    finish(halo(3, pad_middle, 2, pad_middle, 2, 1))
    table = gradients(pad_middle)
    copies = scale_start(1, table)
    linear = back_linear(pad_cot, 0.25 * TIME_STEP, pad_middle, coef_one)
    for comp in range(5):
        linear[comp] = linear[comp] + 0.25 * cotangent[comp]
    inverse_one = scale_finish(1, copies)
    write_features(1, pad_middle, table, inverse_one)
    grad_copies = []
    sweep(both_one, lambda: grad_copies.extend(send_dgradient(1, inverse_one)))
    carried = back_closure(1, inverse_one, linear, grad_copies)
    for comp in range(5):
        pad_carry[comp, 1 : 1 + planes] = carried[comp]

    finish(halo(4, pad_carry, 1, pad_carry, 1, 2))
    write_dstress(pad_carry, TIME_STEP)
    linear = back_linear(pad_carry, TIME_STEP, pad_state, coef_zero)
    for comp in range(5):
        linear[comp] = linear[comp] + (0.75 * cotangent[comp] + shifted(pad_carry, comp, 1, 0))
    grad_copies = []
    sweep(backward_zero, lambda: grad_copies.extend(send_dgradient(0, inverse_zero)))

    factor = 1.0 / (TIME_STEP * CLOSURE_SCALE * math.sqrt(cells))

    def folded(value):
        return (value[:, :hid] + value[:, hid:]) * factor

    both = folded(acc_mid[...])
    mid = both[:hid] + both[hid : 2 * hid]
    narrow = folded(acc_in[...])
    out = folded(acc_out[...])
    rest = jnp.concatenate(
        [
            narrow[:16] + narrow[16:32],
            narrow[32:33],
            both[2 * hid : 2 * hid + 1],
            (out[:16] + out[16:])[2:8],
        ],
        axis=0,
    )
    for slot in range(GROUP):
        grad_parts[slot, 0:8] = mid[8 * slot : 8 * slot + 8]
        if slot < 3:
            grad_parts[slot, 8:16] = rest[8 * slot : 8 * slot + 8]
        else:
            grad_parts[slot, 8:16] = jnp.zeros((8, lanes), F32)
    reduce_copies = [
        remote(
            grad_parts.at[mate(step)],
            grad_slots.at[step],
            red_send.at[step],
            red_recv.at[step],
            base + mate(step),
        )
        for step in range(1, GROUP)
    ]
    result = back_closure(0, inverse_zero, linear, grad_copies)
    for comp in range(5):
        grad_state[comp] = result[comp]
    grad_slots[0] = grad_parts[mine]
    finish(reduce_copies)
    owned = jnp.sum(grad_slots[...], axis=0)
    if far > 1:
        grad_far[0] = owned
        others = [
            remote(
                grad_far.at[0],
                grad_far.at[step],
                far_send.at[2, step],
                far_recv.at[2, step],
                far_mate(step) * GROUP + mine,
            )
            for step in range(1, far)
        ]
        finish(others)
        owned = jnp.sum(grad_far[...], axis=0)
    grad_total[mine] = owned
    gather_copies = [
        remote(
            grad_total.at[mine],
            grad_total.at[mine],
            gat_send.at[step],
            gat_recv.at[step],
            base + mate(step),
        )
        for step in range(1, GROUP)
    ]
    for step, copy in zip(range(1, GROUP), gather_copies):
        copy.wait_send()
        source = mate(GROUP - step)
        pltpu.make_async_remote_copy(
            src_ref=grad_total.at[source],
            dst_ref=grad_total.at[source],
            send_sem=gat_send.at[step],
            recv_sem=gat_recv.at[step],
            device_id={"gx": base + mate(step)},
            device_id_type=MESH,
        ).wait_recv()
    for slot in range(GROUP):
        grad_mid[8 * slot : 8 * slot + 8, :] = grad_total[slot, 0:8]
    grad_in[0:8, :] = grad_total[0, 8:16]
    grad_in[8:16, :] = grad_total[1, 8:16]
    grad_bias_in[...] = grad_total[2, 8:9]
    grad_bias_mid[...] = grad_total[2, 9:10]
    grad_out[...] = grad_total[2, 10:16]


def shards(
    state,
    cotangent,
    weight_in,
    bias_in,
    weight_mid,
    bias_mid,
    weight_out,
    cell_index,
    segment_id,
    segment_coef,
):
    count = lax.axis_size("gx")
    planes, span, lanes = state.shape[1:]
    cells = count * planes * span * lanes
    rows = planes * span
    chunks = rows // ROWS
    wide = ROWS * lanes
    hid = weight_mid.shape[0]
    far = count // GROUP
    dma = pltpu.SemaphoreType.DMA
    vmem = pltpu.VMEM
    tall = (5, planes + 3, span, lanes)
    rim = (planes + 2, span, lanes)
    outs = pl.pallas_call(
        functools.partial(kernel, count, cells),
        out_shape=(
            jax.ShapeDtypeStruct(state.shape, F32),
            jax.ShapeDtypeStruct(weight_in.shape, F32),
            jax.ShapeDtypeStruct((1, hid), F32),
            jax.ShapeDtypeStruct(weight_mid.shape, F32),
            jax.ShapeDtypeStruct((1, hid), F32),
            jax.ShapeDtypeStruct((weight_out.shape[1], hid), F32),
        ),
        in_specs=[pl.BlockSpec(memory_space=pltpu.VMEM)] * 10,
        out_specs=[pl.BlockSpec(memory_space=pltpu.VMEM)] * 6,
        scratch_shapes=[
            vmem(tall, F32),
            vmem(tall, F32),
            vmem(tall, F32),
            vmem(tall, F32),
            vmem((3,) + rim, F32),
            vmem((2, 3) + rim, F32),
            vmem((2, 3, 1, span, lanes), F32),
            vmem((2, 2, 3, 1, span, lanes), F32),
            vmem((2, rows * 16, lanes), F32),
            vmem((rows * 8, lanes), F32),
            vmem((rows * 8, lanes), F32),
            vmem((rows * 16, lanes), F32),
            vmem((chunks, hid, wide), F32),
            vmem((chunks, hid, wide), F32),
            vmem((hid, hid), BF16),
            vmem((2 * hid, 2 * hid), BF16),
            vmem((hid, hid), BF16),
            vmem((32, 2 * hid), BF16),
            vmem((2 * hid, 2 * hid), BF16),
            vmem((32, 2 * hid), BF16),
            vmem((hid, lanes), F32),
            vmem((2 * hid + 16, 2 * hid), F32),
            vmem((48, 2 * hid), F32),
            vmem((32, 2 * hid), F32),
            vmem((2, GROUP, 1, lanes), F32),
            vmem((2, far, 1, lanes), F32),
            vmem((GROUP, 16, lanes), F32),
            vmem((GROUP, 16, lanes), F32),
            vmem((GROUP, 16, lanes), F32),
            vmem((far, 16, lanes), F32),
            dma((7, 2)),
            dma((7, 2)),
            dma((2, GROUP)),
            dma((2, GROUP)),
            dma((GROUP,)),
            dma((GROUP,)),
            dma((GROUP,)),
            dma((GROUP,)),
            dma((3, far)),
            dma((3, far)),
        ],
        compiler_params=pltpu.CompilerParams(
            collective_id=0, has_side_effects=True, vmem_limit_bytes=48 * 1024 * 1024
        ),
        cost_estimate=pl.CostEstimate(
            flops=6 * 2 * 2 * 20000 * rows * lanes, bytes_accessed=2000000, transcendentals=0
        ),
    )(
        state,
        cotangent,
        weight_in,
        bias_in[None],
        weight_mid,
        bias_mid[None],
        weight_out.T,
        cell_index,
        segment_id,
        segment_coef[None],
    )
    return outs[0], outs[1], outs[2][0], outs[3], outs[4][0], outs[5].T


def solution(mesh):
    return jax.shard_map(
        shards,
        mesh=mesh,
        in_specs=(
            P(None, ("grp", "gx"), None, None),
            P(None, ("grp", "gx"), None, None),
            P(),
            P(),
            P(),
            P(),
            P(),
            P(None, "grp"),
            P(None, "grp"),
            P(),
        ),
        out_specs=(
            P(None, ("grp", "gx"), None, None),
            P("grp", None),
            P("grp"),
            P("grp", None),
            P("grp"),
            P("grp", None),
        ),
        check_vma=False,
    )
```

time: 625 us -> 85.4 us (0.14); the launches traced: 614 us -> 85 us
  local copies, waits for them, and re-layouts: 175 us -> 9 us
  matrix products: 165 us -> 0 us
  blocking collectives: 121 us -> 0 us
  Pallas kernels: 0 us -> 75.3 us
  waiting for transfers between devices: 70.7 us -> 0 us
  other arithmetic: 47.9 us -> 0 us
  between operations: 17.7 us -> 0.69 us
  starting transfers between devices: 15.4 us -> 0 us
    dot_general x154 -> x0, matrix products: 165 us -> none  [the longest x56 59.8 us: closure_block(): jnp.dot(weight_mid.T, hidden_one, precision=HIGHEST_PRECISION, preferred_...]
    psum x3 -> x0, blocking collectives: 121 us -> none  [the longest x2 61.3 us: scale_of(): summed = lax.psum(partial_sum, 'gx')]
    pallas_call x0 -> x1, Pallas kernels: none -> 75.3 us  [shards(): pl.pallas_call(functools.partial(kernel, count, cells), out_shape=(jax.Sh...]
    psum x1 -> x0, waiting for transfers between devices: 68.9 us -> none  [shards(): lax.psum((grads_zero[0] + grads_one[0], grads_zero[1] + grads_one[1], gra...]
    unnamed x357 -> x26, local copies, waits for them, and re-layouts: 40.9 us -> 9 us
    dynamic_slice x48 -> x0, local copies, waits for them, and re-layouts: 27.8 us -> none  [subgrid_stress(): stress = lax.map(lambda block: saved(block, weights), feature)]
    split x86 -> x0, local copies, waits for them, and re-layouts: 27.5 us -> none  [the longest x52 15.4 us: along_y(): return (jnp.roll(source, -1, axis=-2) - jnp.roll(source, 1, axis=-2)) * 0.5]
    concatenate x49 -> x0, local copies, waits for them, and re-layouts: 20.7 us -> none  [the longest x29 12.3 us: along_z(): return (jnp.roll(source, -1, axis=-1) - jnp.roll(source, 1, axis=-1)) * 0.5]
  transfers between devices with their start and end apart: 9 -> 0, of which waited for: 2 -> 0; matrix products, arithmetic and copies ran while one was open for 11% -> 0% of each run, Pallas kernels for 0% -> 0%
where the time goes in v1:
time: 85.4 us; the launch traced here: 85 us
  Pallas kernels  75.3 us (88%)
  local copies, waits for them, and re-layouts  9 us (11%)
    pallas_call x1, Pallas kernels, shards(): pl.pallas_call(functools.partial(kernel, count, cells), out_shape=(jax.Sh...  75.3 us
    unnamed x26, local copies, waits for them, and re-layouts  9 us

profile of v1, /device:TPU:0, one launch (start us, length us, event | category | flops | bytes accessed | tf_op | source)
XLA Modules:
  0.0 85.0 jit_solution(11223068608271640712)
XLA Ops:
  0.6 0.0 copy-start.4
  0.6 0.0 copy-start.7
  0.7 0.0 copy-start.8
  0.7 0.0 copy-start.9
  0.7 0.6 copy-done.4
  1.3 0.0 copy-done.7
  1.3 0.0 copy-done.8
  1.3 0.0 copy-done.9
  1.3 0.0 copy-start
  1.3 0.9 %copy-done = f32[5,6,16,128]{3,2,1,0:T(8,128)S(1)} copy-done((f32[5,6,16,128]{3,2,1,0:T(8,128)S(1)}, f32[5,6,16,128]{3,2,1,0:T(8,128)}, u32[]{:S(2)}) %copy-start) | copy-done | bytes 245784
  2.3 0.0 copy-start.1
  2.3 0.9 %copy-done.1 = f32[5,6,16,128]{3,2,1,0:T(8,128)S(1)} copy-done((f32[5,6,16,128]{3,2,1,0:T(8,128)S(1)}, f32[5,6,16,128]{3,2,1,0:T(8,128)}, u32[]{:S(2)}) %copy-start.1) | copy-done | bytes 245784
  3.2 0.0 copy-start.2
  3.2 0.8 copy-done.2
  4.1 0.0 copy-start.3
  4.1 0.7 copy-done.3
  4.8 0.0 copy-start.5
  4.8 0.7 copy-done.5
  5.5 0.0 copy-start.6
  5.5 0.7 copy-done.6
  6.1 75.3 %shard_map.145 = (f32[5,6,16,128]{3,2,1,0:T(8,128)S(1)}, f32[16,128]{1,0:T(8,128)S(1)}, f32[1,128]{1,0:T(1,128)S(1)}, f32[128,128]{1,0:T(8,128)S(1)}, f32[1,128]{1,0:T(1,128)S(1)}, /*index=5*/f32[6,128]{1,0:T(8,128)S(1)}) custom-call(f32[5,6,16,128]{3,2,1,0:T(8,128)S(1)} %copy-done, f32[5,6,16,128]{3,2,1,0:T(8,128)S(1)} %copy-done.1, ...), custom_call_target="tpu_custom_call" | custom-call | flops 5898240000 | bytes 2000000 | tf_op jit(solution)/shard_map/pallas_call | solution.py:672
  81.5 0.7 copy.22
  82.2 0.6 copy.23
  82.8 0.5 copy.24
  83.3 0.6 copy.25
  83.9 0.5 copy.26
  84.4 0.6 copy.27
Async XLA Ops:
  0.6 0.7 copy-start.4
  0.6 0.7 copy-start.7
  0.7 0.7 copy-start.8
  0.7 0.7 copy-start.9
  1.3 0.9 %copy-start = (f32[5,6,16,128]{3,2,1,0:T(8,128)S(1)}, f32[5,6,16,128]{3,2,1,0:T(8,128)}, u32[]{:S(2)}) copy-start(f32[5,6,16,128]{3,2,1,0:T(8,128)} %state.1) | copy-start | bytes 737284
  2.3 0.9 %copy-start.1 = (f32[5,6,16,128]{3,2,1,0:T(8,128)S(1)}, f32[5,6,16,128]{3,2,1,0:T(8,128)}, u32[]{:S(2)}) copy-start(f32[5,6,16,128]{3,2,1,0:T(8,128)} %cotangent.1) | copy-start | bytes 737284
  3.2 0.8 copy-start.2
  4.1 0.7 copy-start.3
  4.8 0.7 copy-start.5
  5.5 0.7 copy-start.6

commit v2 on v1

--- a/solution.py
+++ b/solution.py
@@ -14,7 +14,7 @@
 EPSILON = 1e-05
 F32 = jnp.float32
 BF16 = jnp.bfloat16
-ROWS = 8
+ROWS = 16
 GROUP = 16
 MESH = pl.DeviceIdType.MESH
 
@@ -65,8 +65,13 @@
     pad_carry,
     pad_stress,
     pad_grad,
-    send_stress,
+    send_mid,
+    recv_mid,
     send_grad,
+    send_high,
+    send_low,
+    recv_low,
+    recv_high,
     feats,
     stress,
     dstress,
@@ -393,20 +398,21 @@
         two_parts = jnp.concatenate(split(two), axis=0)
         backward(chunk, feat, one, one_parts, two, two_parts)
 
-    def sweep(body, between):
-        edge = 2 * per_plane
+    def sweep(body, between, first, last):
+        first, last = first * per_plane, last * per_plane
+        chunks = planes * per_plane
 
         def outer(step, carry):
-            body(jnp.where(step < per_plane, step, step + (planes - 2) * per_plane))
+            body(jnp.where(step < first, step, step + (chunks - first - last)))
             return carry
 
         def inner(step, carry):
             body(step)
             return carry
 
-        lax.fori_loop(0, edge, outer, 0)
+        lax.fori_loop(0, first + last, outer, 0)
         between()
-        lax.fori_loop(per_plane, (planes - 1) * per_plane, inner, 0)
+        lax.fori_loop(first, chunks - last, inner, 0)
 
     def upwind(ref, comp):
         return (
@@ -445,17 +451,35 @@
             total = total + (here - there) * get(dfeats, 15, 16, plane, number)
         return total * inverse
 
-    def send_dgradient(section, inverse):
+    def send_dgradient():
         for a in range(3):
-            send_grad[section, 0, a] = dgradient(section, a, 0, inverse, planes - 1, 1)
-            send_grad[section, 1, a] = dgradient(section, a, 0, inverse, 0, 1)
+            send_grad[0, a] = dgradient(0, a, 0, inverse_zero, planes - 1, 1)
+            send_grad[1, a] = dgradient(0, a, 0, inverse_zero, 0, 1)
         return exchange(
-            5 + section,
-            send_grad.at[section, 0],
-            pad_grad.at[section, :, 0:1],
-            send_grad.at[section, 1],
-            pad_grad.at[section, :, planes + 1 : planes + 2],
-        )
+            6,
+            send_grad.at[0],
+            pad_grad.at[0, :, 0:1],
+            send_grad.at[1],
+            pad_grad.at[0, :, planes + 1 : planes + 2],
+        )
+
+    def send_carry():
+        top = closure_local(1, inverse_one, linear, planes - 1, 1)
+        low = closure_local(1, inverse_one, linear, 0, 2)
+        for a in range(3):
+            start = dgradient(1, a, 0, inverse_one, 0, 3)
+            end = dgradient(1, a, 0, inverse_one, planes - 2, 2)
+            send_high[a] = end[1]
+            send_low[a] = start[0]
+            top[1 + a] = top[1 + a] + 0.5 * end[0:1]
+            send_low[3 + 2 * (1 + a)] = low[1 + a][0] - 0.5 * start[1]
+            send_low[4 + 2 * (1 + a)] = low[1 + a][1] - 0.5 * (start[2] - start[0])
+        for comp in range(5):
+            send_high[3 + comp] = top[comp][0]
+        for comp in (0, 4):
+            send_low[3 + 2 * comp] = low[comp][0]
+            send_low[4 + 2 * comp] = low[comp][1]
+        return exchange(5, send_high, recv_low, send_low, recv_high)
 
     def back_linear(ref, factor, speed_ref, coef):
         mass_rho = shifted(ref, 0, 1, 0) + shifted(ref, 4, 1, 0)
@@ -470,19 +494,23 @@
             (upwind_back(ref, 4) + along_x(ref, 1, 1) + along_y(v) + along_z(w)) * factor,
         ]
 
-    def back_closure(section, inverse, linear, copies):
-        for a in range(3):
-            pad_grad[section, a, 1 : 1 + planes] = dgradient(section, a, 0, inverse, 0, planes)
-        total = list(linear)
+    def closure_local(section, inverse, linear, plane, number):
+        total = [entry[plane : plane + number] for entry in linear]
         for slot, comp in enumerate((1, 2, 3, 0, 4)):
-            total[comp] = total[comp] + get(dfeats, 9 + slot, 16)
+            total[comp] = total[comp] + get(dfeats, 9 + slot, 16, plane, number)
         for a in range(3):
             total[1 + a] = (
                 total[1 + a]
-                - along_y(dgradient(section, a, 1, inverse, 0, planes))
-                - along_z(dgradient(section, a, 2, inverse, 0, planes))
+                - along_y(dgradient(section, a, 1, inverse, plane, number))
+                - along_z(dgradient(section, a, 2, inverse, plane, number))
             )
-        finish(copies)
+        return total
+
+    def back_closure(section, inverse, linear, arrive):
+        for a in range(3):
+            pad_grad[section, a, 1 : 1 + planes] = dgradient(section, a, 0, inverse, 0, planes)
+        total = closure_local(section, inverse, linear, 0, planes)
+        arrive()
         ref = pad_grad.at[section]
         for a in range(3):
             total[1 + a] = total[1 + a] - along_x(ref, a, 1)
@@ -510,35 +538,51 @@
     inverse_zero = scale_finish(0, copies)
     write_features(0, pad_state, table, inverse_zero)
     stress_copies = []
+    gain = TIME_STEP * CLOSURE_SCALE
+
+    def stress_terms(plane, number):
+        s_yy, s_zz, s_xy, s_xz, s_yz = (
+            get(stress, 2 + entry, 8, plane, number) for entry in (1, 2, 3, 4, 5)
+        )
+        return (
+            along_y(s_xy) + along_z(s_xz),
+            along_y(s_yy) + along_z(s_yz),
+            along_y(s_yz) + along_z(s_zz),
+        )
 
     def send_edges():
+        top = stress_terms(planes - 1, 1)
+        low = stress_terms(0, 1)
         for slot, entry in enumerate((0, 3, 4)):
-            send_stress[0, slot] = get(stress, 2 + entry, 8, planes - 1, 1)
-            send_stress[1, slot] = get(stress, 2 + entry, 8, 0, 1)
+            end = get(stress, 2 + entry, 8, planes - 2, 2)
+            start = get(stress, 2 + entry, 8, 0, 2)
+            send_mid[0, slot] = end[1]
+            send_mid[1, slot] = start[0]
+            send_mid[0, 3 + slot] = pad_middle[1 + slot, 1 + planes] + gain * (
+                top[slot][0] - 0.5 * end[0]
+            )
+            send_mid[1, 3 + slot] = pad_middle[1 + slot, 2] + gain * (low[slot][0] + 0.5 * start[1])
         stress_copies.extend(
-            exchange(
-                2,
-                send_stress.at[0],
-                pad_stress.at[:, 0:1],
-                send_stress.at[1],
-                pad_stress.at[:, planes + 1 : planes + 2],
-            )
-        )
-
-    sweep(forward_zero, send_edges)
+            exchange(2, send_mid.at[0], recv_mid.at[0], send_mid.at[1], recv_mid.at[1])
+        )
+
+    sweep(forward_zero, send_edges, 2, 2)
     for slot, entry in enumerate((0, 3, 4)):
         pad_stress[slot, 1 : 1 + planes] = get(stress, 2 + entry, 8)
-    s_yy, s_zz, s_xy, s_xz, s_yz = (get(stress, 2 + entry, 8) for entry in (1, 2, 3, 4, 5))
-    sub_x = along_y(s_xy) + along_z(s_xz)
-    sub_y = along_y(s_yy) + along_z(s_yz)
-    sub_z = along_y(s_yz) + along_z(s_zz)
+    subs = stress_terms(0, planes)
     finish(stress_copies)
-    gain = TIME_STEP * CLOSURE_SCALE
-    for slot, sub in enumerate((sub_x, sub_y, sub_z)):
+    for slot in range(3):
+        pad_stress[slot, 0] = recv_mid[0, slot]
+        pad_stress[slot, planes + 1] = recv_mid[1, slot]
         here = shifted(pad_middle, 1 + slot, 2, 0)
-        pad_middle[1 + slot, 2 : 2 + planes] = here + gain * (sub + along_x(pad_stress, slot, 1))
-
-    finish(halo(3, pad_middle, 2, pad_middle, 2, 1))
+        pad_middle[1 + slot, 2 : 2 + planes] = here + gain * (
+            subs[slot] + along_x(pad_stress, slot, 1)
+        )
+        pad_middle[1 + slot, 1] = recv_mid[0, 3 + slot] + 0.5 * gain * pad_stress[slot, 1]
+        pad_middle[1 + slot, 2 + planes] = (
+            recv_mid[1, 3 + slot] - 0.5 * gain * pad_stress[slot, planes]
+        )
+
     table = gradients(pad_middle)
     copies = scale_start(1, table)
     linear = back_linear(pad_cot, 0.25 * TIME_STEP, pad_middle, coef_one)
@@ -547,18 +591,33 @@
     inverse_one = scale_finish(1, copies)
     write_features(1, pad_middle, table, inverse_one)
     grad_copies = []
-    sweep(both_one, lambda: grad_copies.extend(send_dgradient(1, inverse_one)))
-    carried = back_closure(1, inverse_one, linear, grad_copies)
+    carry_copies = []
+    sweep(both_one, lambda: carry_copies.extend(send_carry()), 3, 2)
+
+    def carry_arrives():
+        finish(carry_copies)
+        for a in range(3):
+            pad_grad[1, a, 0] = recv_low[a]
+            pad_grad[1, a, planes + 1] = recv_high[a]
+
+    carried = back_closure(1, inverse_one, linear, carry_arrives)
     for comp in range(5):
         pad_carry[comp, 1 : 1 + planes] = carried[comp]
-
-    finish(halo(4, pad_carry, 1, pad_carry, 1, 2))
+        low = recv_low[3 + comp]
+        top = recv_high[3 + 2 * comp]
+        if 1 <= comp <= 3:
+            low = low - 0.5 * pad_grad[1, comp - 1, 1]
+            top = top + 0.5 * pad_grad[1, comp - 1, planes]
+        pad_carry[comp, 0] = low
+        pad_carry[comp, 1 + planes] = top
+        pad_carry[comp, 2 + planes] = recv_high[4 + 2 * comp]
+
     write_dstress(pad_carry, TIME_STEP)
     linear = back_linear(pad_carry, TIME_STEP, pad_state, coef_zero)
     for comp in range(5):
         linear[comp] = linear[comp] + (0.75 * cotangent[comp] + shifted(pad_carry, comp, 1, 0))
     grad_copies = []
-    sweep(backward_zero, lambda: grad_copies.extend(send_dgradient(0, inverse_zero)))
+    sweep(backward_zero, lambda: grad_copies.extend(send_dgradient()), 1, 1)
 
     factor = 1.0 / (TIME_STEP * CLOSURE_SCALE * math.sqrt(cells))
 
@@ -594,7 +653,7 @@
         )
         for step in range(1, GROUP)
     ]
-    result = back_closure(0, inverse_zero, linear, grad_copies)
+    result = back_closure(0, inverse_zero, linear, lambda: finish(grad_copies))
     for comp in range(5):
         grad_state[comp] = result[comp]
     grad_slots[0] = grad_parts[mine]
@@ -688,8 +747,13 @@
             vmem(tall, F32),
             vmem((3,) + rim, F32),
             vmem((2, 3) + rim, F32),
+            vmem((2, 6, span, lanes), F32),
+            vmem((2, 6, span, lanes), F32),
             vmem((2, 3, 1, span, lanes), F32),
-            vmem((2, 2, 3, 1, span, lanes), F32),
+            vmem((8, span, lanes), F32),
+            vmem((13, span, lanes), F32),
+            vmem((8, span, lanes), F32),
+            vmem((13, span, lanes), F32),
             vmem((2, rows * 16, lanes), F32),
             vmem((rows * 8, lanes), F32),
             vmem((rows * 8, lanes), F32),

time: 85.4 us -> 73.9 us (0.87)
  Pallas kernels: 75.3 us -> 63.8 us
    pallas_call x1, Pallas kernels: 75.3 us -> 63.8 us  [shards(): pl.pallas_call(functools.partial(kernel, count, cells), out_shape=(jax.Sh...]
where the time goes in v2:
time: 73.9 us; the launch traced here: 73.5 us
  Pallas kernels  63.8 us (86%)
  local copies, waits for them, and re-layouts  9 us (12%)
    pallas_call x1, Pallas kernels, shards(): pl.pallas_call(functools.partial(kernel, count, cells), out_shape=(jax.Sh...  63.8 us
    unnamed x26, local copies, waits for them, and re-layouts  9 us

profile of v2, /device:TPU:0, one launch (start us, length us, event | category | flops | bytes accessed | tf_op | source)
XLA Modules:
  0.0 73.5 jit_solution(45356168157169147)
XLA Ops:
  0.6 0.0 copy-start.4
  0.6 0.0 copy-start.7
  0.7 0.0 copy-start.8
  0.7 0.0 copy-start.9
  0.7 0.6 copy-done.4
  1.3 0.0 copy-done.7
  1.3 0.0 copy-done.8
  1.3 0.0 copy-done.9
  1.3 0.0 copy-start
  1.3 0.9 %copy-done = f32[5,6,16,128]{3,2,1,0:T(8,128)S(1)} copy-done((f32[5,6,16,128]{3,2,1,0:T(8,128)S(1)}, f32[5,6,16,128]{3,2,1,0:T(8,128)}, u32[]{:S(2)}) %copy-start) | copy-done | bytes 245784
  2.3 0.0 copy-start.1
  2.3 0.9 %copy-done.1 = f32[5,6,16,128]{3,2,1,0:T(8,128)S(1)} copy-done((f32[5,6,16,128]{3,2,1,0:T(8,128)S(1)}, f32[5,6,16,128]{3,2,1,0:T(8,128)}, u32[]{:S(2)}) %copy-start.1) | copy-done | bytes 245784
  3.2 0.0 copy-start.2
  3.2 0.8 %copy-done.2 = f32[128,128]{1,0:T(8,128)S(1)} copy-done((f32[128,128]{1,0:T(8,128)S(1)}, f32[128,128]{1,0:T(8,128)}, u32[]{:S(2)}) %copy-start.2) | copy-done | bytes 65560
  4.1 0.0 copy-start.3
  4.1 0.7 copy-done.3
  4.8 0.0 copy-start.5
  4.8 0.7 copy-done.5
  5.5 0.0 copy-start.6
  5.5 0.7 copy-done.6
  6.1 63.8 %shard_map.145 = (f32[5,6,16,128]{3,2,1,0:T(8,128)S(1)}, f32[16,128]{1,0:T(8,128)S(1)}, f32[1,128]{1,0:T(1,128)S(1)}, f32[128,128]{1,0:T(8,128)S(1)}, f32[1,128]{1,0:T(1,128)S(1)}, /*index=5*/f32[6,128]{1,0:T(8,128)S(1)}) custom-call(f32[5,6,16,128]{3,2,1,0:T(8,128)S(1)} %copy-done, f32[5,6,16,128]{3,2,1,0:T(8,128)S(1)} %copy-done.1, ...), custom_call_target="tpu_custom_call" | custom-call | flops 5898240000 | bytes 2000000 | tf_op jit(solution)/shard_map/pallas_call | solution.py:731
  70.0 0.7 copy.22
  70.7 0.6 copy.23
  71.3 0.5 copy.24
  71.8 0.6 copy.25
  72.4 0.5 copy.26
  72.9 0.6 copy.27
Async XLA Ops:
  0.6 0.7 copy-start.4
  0.6 0.7 copy-start.7
  0.7 0.7 copy-start.8
  0.7 0.7 copy-start.9
  1.3 0.9 %copy-start = (f32[5,6,16,128]{3,2,1,0:T(8,128)S(1)}, f32[5,6,16,128]{3,2,1,0:T(8,128)}, u32[]{:S(2)}) copy-start(f32[5,6,16,128]{3,2,1,0:T(8,128)} %state.1) | copy-start | bytes 737284
  2.3 0.9 %copy-start.1 = (f32[5,6,16,128]{3,2,1,0:T(8,128)S(1)}, f32[5,6,16,128]{3,2,1,0:T(8,128)}, u32[]{:S(2)}) copy-start(f32[5,6,16,128]{3,2,1,0:T(8,128)} %cotangent.1) | copy-start | bytes 737284
  3.2 0.8 %copy-start.2 = (f32[128,128]{1,0:T(8,128)S(1)}, f32[128,128]{1,0:T(8,128)}, u32[]{:S(2)}) copy-start(f32[128,128]{1,0:T(8,128)} %weight_mid.1) | copy-start | bytes 196612
  4.1 0.7 copy-start.3
  4.8 0.7 copy-start.5
  5.5 0.7 copy-start.6
